TPU v7x, 256 devices: a whole 4x4x8 slice. The times are simulated.
256 devices in a mesh: dp: 2 (over y_hi), row: 8 (over z), col: 16 (over x, y_lo, core).
Axes of the slice: x: 4, y: 4 (y_hi: 2, y_lo: 2; y = y_hi * 2 + y_lo), z: 8, core: 2. Of those that a mesh axis runs over, the one named last changes fastest.
Arguments:
- partials: float32 [2, 8192, 28672], P('dp', ('row', 'col')), may hold values from -22.5 to 22.5
- clip_ratio: float32 [1], replicated, may hold values from 0.5 to 1
- start_block: float32 [28672, 128], P(('dp', 'col')), may hold values from -1 to 1
Outputs:
- update: float32 [8192, 28672], P(('row', 'col'), 'dp')
- basis: float32 [28672, 128], P(('dp', 'col'))
All inputs are finite; a program needn't handle non-finite values.
Results may differ from a plain program's by a relative error of at most 0.0002.
Values sent between devices are 32-bit elements; how exact they have to be, the bound alone decides.
A program may use at most 128 MiB of HBM per device.

v0:
```python
import math

import jax
import jax.numpy as jnp
from jax import lax
from jax.sharding import PartitionSpec as P

M = 8192
N = 28672
K = 128
ITERS = 3


def orthonormal(block, gram):
    factor = jnp.linalg.cholesky(gram)
    return jax.scipy.linalg.solve_triangular(factor, block.T, lower=True).T


def times_tile(tile, block):
    return jnp.dot(tile, block, precision=lax.Precision.HIGHEST, preferred_element_type=jnp.float32)


def tile_transposed(tile, block):
    return lax.dot_general(
        tile,
        block,
        (((0,), (0,)), ((), ())),
        precision=lax.Precision.HIGHEST,
        preferred_element_type=jnp.float32,
    )


def gram_of(block):
    return jnp.dot(
        block.T, block, precision=lax.Precision.HIGHEST, preferred_element_type=jnp.float32
    )


def body(partials, clip_ratio, start_block):
    summed = lax.psum_scatter(partials[0], "dp", scatter_dimension=1, tiled=True)
    tile = lax.all_to_all(summed, "col", split_axis=1, concat_axis=0, tiled=True)
    vectors = start_block * math.sqrt(3.0 / N)
    second = jnp.zeros((K, K), jnp.float32)
    for step in range(ITERS):
        left = lax.psum(times_tile(tile, vectors), ("dp", "col"))
        gram = lax.psum(gram_of(left), "row")
        basis_left = orthonormal(left, gram)
        right = lax.psum(tile_transposed(tile, basis_left), "row")
        second = lax.psum(gram_of(right), ("dp", "col"))
        vectors = orthonormal(right, second)
    sigma = jnp.sqrt(jnp.sqrt(jnp.sum(second * second)))
    limit = clip_ratio[0] * (math.sqrt(M) + math.sqrt(N))
    scale = limit / sigma
    update = summed * scale
    return (update, vectors)


def solution(mesh):
    placed = (P("dp", ("row", "col"), None), P(), P(("dp", "col"), None))
    return jax.shard_map(
        body,
        mesh=mesh,
        in_specs=placed,
        out_specs=(P(("row", "col"), "dp"), P(("dp", "col"), None)),
        check_vma=False,
    )
```

profile of v0, /device:TPU:1, one launch (start us, length us, event | category | flops | bytes accessed | tf_op | source)
XLA Modules:
  0.0 1466.6 jit_solution(2468238942680946773)
XLA Ops:
  7.9 101.5 %reduce-scatter.2.cloned.1.call-done = f32[64,14336]{1,0:T(8,128)} async-done(((f32[64,28672]{1,0:T(8,128)}), f32[64,14336]{1,0:T(8,128)}) %reduce-scatter.2.cloned.1.call-update) | async-done | bytes 3670032 | tf_op jit(solution)/shard_map/reduce_scatter | solution.py:40
  111.9 48.2 %all_to_all.19 = f32[64,16,896]{2,0,1:T(8,128)S(1)} all-to-all(f32[64,16,896]{2,0,1:T(8,128)S(1)} %bitcast.124), channel_id=1, replica_groups=mesh['dp'=2,'row'=8,'col'=16] {'col'}, dimensions={1} | all-to-all | bytes 7340032 | tf_op jit(solution)/shard_map/all_to_all | solution.py:41
  161.9 4.8 convolution_bitcast_fusion.2
  166.8 112.6 %all-reduce.13.cloned.1.call-done = f32[1024,128]{0,1:T(8,128)} async-done(((f32[1024,128]{0,1:T(8,128)}), f32[1024,128]{0,1:T(8,128)}) %all-reduce.13.cloned.1.call-update) | async-done | bytes 524304 | tf_op jit(solution)/shard_map/psum | solution.py:45
  282.0 66.3 %all-reduce.15.cloned.1.call-done = f32[128,128]{0,1:T(8,128)} async-done(((f32[128,128]{0,1:T(8,128)}), f32[128,128]{0,1:T(8,128)}) %all-reduce.15.cloned.1.call-update) | async-done | bytes 65552 | tf_op jit(solution)/shard_map/psum | solution.py:46
  350.2 11.7 cholesky.104
  363.2 9.8 custom-call.12
  374.7 5.1 convolution_bitcast_fusion.5
  379.8 72.2 %all-reduce.17.cloned.1.call-done = f32[896,128]{0,1:T(8,128)} async-done(((f32[896,128]{0,1:T(8,128)}), f32[896,128]{0,1:T(8,128)}) %all-reduce.17.cloned.1.call-update) | async-done | bytes 458768 | tf_op jit(solution)/shard_map/psum | solution.py:48
  454.7 110.0 %all-reduce.19.cloned.1.call-done = f32[128,128]{0,1:T(8,128)} async-done(((f32[128,128]{0,1:T(8,128)}), f32[128,128]{0,1:T(8,128)}) %all-reduce.19.cloned.1.call-update) | async-done | bytes 65552 | tf_op jit(solution)/shard_map/psum | solution.py:49
  566.5 11.7 cholesky.115
  579.6 9.8 custom-call.13
  591.0 6.7 convolution_bitcast_fusion.1
  597.7 112.3 %all-reduce.21.cloned.1.call-done = f32[1024,128]{0,1:T(8,128)} async-done(((f32[1024,128]{0,1:T(8,128)}), f32[1024,128]{0,1:T(8,128)}) %all-reduce.21.cloned.1.call-update) | async-done | bytes 524304 | tf_op jit(solution)/shard_map/psum | solution.py:45
  712.9 66.1 %all-reduce.23.cloned.1.call-done = f32[128,128]{0,1:T(8,128)} async-done(((f32[128,128]{0,1:T(8,128)}), f32[128,128]{0,1:T(8,128)}) %all-reduce.23.cloned.1.call-update) | async-done | bytes 65552 | tf_op jit(solution)/shard_map/psum | solution.py:46
  780.8 11.7 cholesky.126
  793.9 9.8 custom-call.14
  805.4 5.1 convolution_bitcast_fusion.4
  810.5 72.2 %all-reduce.25.cloned.1.call-done = f32[896,128]{0,1:T(8,128)} async-done(((f32[896,128]{0,1:T(8,128)}), f32[896,128]{0,1:T(8,128)}) %all-reduce.25.cloned.1.call-update) | async-done | bytes 458768 | tf_op jit(solution)/shard_map/psum | solution.py:48
  885.3 110.2 %all-reduce.27.cloned.1.call-done = f32[128,128]{0,1:T(8,128)} async-done(((f32[128,128]{0,1:T(8,128)}), f32[128,128]{0,1:T(8,128)}) %all-reduce.27.cloned.1.call-update) | async-done | bytes 65552 | tf_op jit(solution)/shard_map/psum | solution.py:49
  997.3 11.7 cholesky.137
  1010.4 9.8 custom-call.15
  1021.8 6.7 convolution_bitcast_fusion
  1028.5 112.3 %all-reduce.29.cloned.1.call-done = f32[1024,128]{0,1:T(8,128)} async-done(((f32[1024,128]{0,1:T(8,128)}), f32[1024,128]{0,1:T(8,128)}) %all-reduce.29.cloned.1.call-update) | async-done | bytes 524304 | tf_op jit(solution)/shard_map/psum | solution.py:45
  1143.5 66.3 %all-reduce.31.cloned.1.call-done = f32[128,128]{0,1:T(8,128)} async-done(((f32[128,128]{0,1:T(8,128)}), f32[128,128]{0,1:T(8,128)}) %all-reduce.31.cloned.1.call-update) | async-done | bytes 65552 | tf_op jit(solution)/shard_map/psum | solution.py:46
  1211.6 11.7 cholesky.148
  1224.7 9.8 custom-call.16
  1236.2 5.1 convolution_bitcast_fusion.3
  1241.5 72.0 %all-reduce.33.cloned.1.call-done = f32[896,128]{0,1:T(8,128)} async-done(((f32[896,128]{0,1:T(8,128)}), f32[896,128]{0,1:T(8,128)}) %all-reduce.33.cloned.1.call-update) | async-done | bytes 458768 | tf_op jit(solution)/shard_map/psum | solution.py:48
  1316.6 109.7 %all-reduce.35.cloned.1.call-done = f32[128,128]{0,1:T(8,128)} async-done(((f32[128,128]{0,1:T(8,128)}), f32[128,128]{0,1:T(8,128)}) %all-reduce.35.cloned.1.call-update) | async-done | bytes 65552 | tf_op jit(solution)/shard_map/psum | solution.py:49
  1428.1 11.7 cholesky.159
  1441.1 9.8 custom-call.17
  (76 shorter events, 56.5 us)
Async XLA Ops:
  7.2 102.3 %reduce-scatter.2.cloned.1.call-start = ((), (), s32[]{:S(2)}) async-start(), calls=%async_computation.2 | async-start | bytes 11010048 | tf_op jit(solution)/shard_map/reduce_scatter | solution.py:40
  7.9 271.5 %all-reduce.13.cloned.1.call-start = ((), (), s32[]{:S(2)}) async-start(), calls=%async_computation.3 | async-start | bytes 1048576 | tf_op jit(solution)/shard_map/psum | solution.py:45
  111.9 50.1 %copy-start.1 = (f32[896,128]{1,0:T(8,128)S(1)}, f32[896,128]{1,0:T(8,128)}, u32[]{:S(2)}) copy-start(f32[896,128]{1,0:T(8,128)} %param.10) | copy-start | bytes 1376260
  160.1 1.8 copy-start
  166.7 181.7 %all-reduce.15.cloned.1.call-start = ((), (), s32[]{:S(2)}) async-start(), calls=%async_computation.4 | async-start | bytes 131072 | tf_op jit(solution)/shard_map/psum | solution.py:46
  281.8 170.2 %all-reduce.17.cloned.1.call-start = ((), (), s32[]{:S(2)}) async-start(), calls=%async_computation.5 | async-start | bytes 917504 | tf_op jit(solution)/shard_map/psum | solution.py:48
  379.8 184.9 %all-reduce.19.cloned.1.call-start = ((), (), s32[]{:S(2)}) async-start(), calls=%async_computation.6 | async-start | bytes 131072 | tf_op jit(solution)/shard_map/psum | solution.py:49
  454.4 255.6 %all-reduce.21.cloned.1.call-start = ((), (), s32[]{:S(2)}) async-start(), calls=%async_computation.7 | async-start | bytes 1048576 | tf_op jit(solution)/shard_map/psum | solution.py:45
  597.7 181.3 %all-reduce.23.cloned.1.call-start = ((), (), s32[]{:S(2)}) async-start(), calls=%async_computation.8 | async-start | bytes 131072 | tf_op jit(solution)/shard_map/psum | solution.py:46
  712.5 170.2 %all-reduce.25.cloned.1.call-start = ((), (), s32[]{:S(2)}) async-start(), calls=%async_computation.9 | async-start | bytes 917504 | tf_op jit(solution)/shard_map/psum | solution.py:48
  810.4 185.1 %all-reduce.27.cloned.1.call-start = ((), (), s32[]{:S(2)}) async-start(), calls=%async_computation.10 | async-start | bytes 131072 | tf_op jit(solution)/shard_map/psum | solution.py:49
  885.1 255.8 %all-reduce.29.cloned.1.call-start = ((), (), s32[]{:S(2)}) async-start(), calls=%async_computation.11 | async-start | bytes 1048576 | tf_op jit(solution)/shard_map/psum | solution.py:45
  1028.5 181.3 %all-reduce.31.cloned.1.call-start = ((), (), s32[]{:S(2)}) async-start(), calls=%async_computation.12 | async-start | bytes 131072 | tf_op jit(solution)/shard_map/psum | solution.py:46
  1143.3 170.2 %all-reduce.33.cloned.1.call-start = ((), (), s32[]{:S(2)}) async-start(), calls=%async_computation.13 | async-start | bytes 917504 | tf_op jit(solution)/shard_map/psum | solution.py:48
  1241.2 185.1 %all-reduce.35.cloned.1.call-start = ((), (), s32[]{:S(2)}) async-start(), calls=%async_computation.14 | async-start | bytes 131072 | tf_op jit(solution)/shard_map/psum | solution.py:49
Sparse Core Ops, SparseCore 0:
  10.6 98.8 reduce-scatter.1
  166.8 112.5 all-reduce.12
  282.3 66.0 all-reduce.14
  379.9 72.0 all-reduce.16
  455.7 108.9 all-reduce.18
  597.8 112.2 all-reduce.20
  712.9 66.0 all-reduce.22
  810.6 72.0 all-reduce.24
  886.5 108.9 all-reduce.26
  1028.6 112.1 all-reduce.28
  1143.7 66.0 all-reduce.30
  1241.4 72.0 all-reduce.32
  1317.3 108.9 all-reduce.34
where the time goes:
time: 1470 us
  waiting for transfers between devices  1180 us (80%)
  other arithmetic  148 us (10%)
  matrix products  57.4 us (4%)
  blocking collectives  48.2 us (3%)
  between operations  15.7 us (1%)
    psum x3, waiting for transfers between devices, body(): left = lax.psum(times_tile(tile, vectors), ('dp', 'col'))  337 us
    psum x3, waiting for transfers between devices, body(): second = lax.psum(gram_of(right), ('dp', 'col'))  330 us
    psum x3, waiting for transfers between devices, body(): right = lax.psum(tile_transposed(tile, basis_left), 'row')  216 us
    psum x3, waiting for transfers between devices, body(): gram = lax.psum(gram_of(left), 'row')  199 us
    reduce_scatter x1, waiting for transfers between devices, body(): lax.psum_scatter(partials[0], 'dp', scatter_dimension=1, tiled=True)  101 us
    another operation x18, other arithmetic, orthonormal(): factor = jnp.linalg.cholesky(gram)  74.3 us
    another operation x12, other arithmetic, orthonormal(): return jax.scipy.linalg.solve_triangular(factor, block.T, lower=True).T  62.8 us
    all_to_all x1, blocking collectives, body(): lax.all_to_all(summed, 'col', split_axis=1, concat_axis=0, tiled=True)  48.2 us
  transfers between devices with their start and end apart: 13, of which 13 were waited for; matrix products, arithmetic and copies ran while one was open for 0% of the time, Pallas kernels for 0%

commit v1 on v0

v1 whole, which is shorter than its diff:
```python
import math

import jax
import jax.numpy as jnp
from jax import lax
from jax.experimental import pallas as pl
from jax.experimental.pallas import tpu as pltpu
from jax.sharding import PartitionSpec as P

M = 8192
N = 28672
K = 128
ITERS = 3
TR = 1024
TC = 896
ZB = 112
MESH = pl.DeviceIdType.MESH
BF = jnp.bfloat16
F32 = jnp.float32

G2_CORE, G2_X, G2_Y, G2_XG, G2_CG = 0, 1, 5, 9, 13
L_CORE, L_X, L_Y, L_XG, L_CG = 14, 15, 19, 23, 27
G1_RS, G1_AG, W_RS, W_AG = 28, 36, 44, 52
SEMS = 60


def split2(a):
    hi = a.astype(BF)
    return hi, (a - hi.astype(F32)).astype(BF)


def dot_f32(a, b, dims):
    return lax.dot_general(a, b, (dims, ((), ())), preferred_element_type=F32)


def wide(a):
    hi, lo = split2(a)
    return jnp.concatenate([hi, lo], axis=1)


def full_dot(a, b, dims):
    return lax.dot_general(
        a, b, (dims, ((), ())), precision=lax.Precision.HIGHEST, preferred_element_type=F32
    )


def split_product(hi, lo, both):
    first = jnp.dot(hi, both, preferred_element_type=F32)
    return first[:, :K] + first[:, K:] + jnp.dot(lo, both[:, :K], preferred_element_type=F32)


def inverse_factor(gram):
    lane = lax.broadcasted_iota(jnp.int32, (8, K), 1)
    sub = lax.broadcasted_iota(jnp.int32, (8, K), 0)
    col = lax.broadcasted_iota(jnp.int32, (K, K), 1)
    row = lax.broadcasted_iota(jnp.int32, (K, K), 0)

    def step(k, x):
        p = x[0:8, :]
        q = jnp.where(lane == sub, 1.0, 0.0).astype(F32)
        for j in range(8):
            piv = p[j : j + 1, j : j + 1]
            rs = lax.rsqrt(piv)
            rs = rs * (1.5 - 0.5 * piv * rs * rs)
            urow = p[j : j + 1, :] * rs
            qrow = q[j : j + 1, :] * rs
            m = jnp.where(sub > j, p[:, j : j + 1] * rs, 0.0)
            p = jnp.where(sub == j, urow, p - m * urow)
            q = jnp.where(sub == j, qrow, q - m * qrow)
        y = jnp.where(lane < 8, q, p)
        left = jnp.where((lane >= 8) & (lane < K - 8 * k), p, 0.0)

        def split3(a):
            hi = a.astype(BF).astype(F32)
            mid = (a - hi).astype(BF).astype(F32)
            return hi, mid, a - hi - mid

        lh, lm, ll = split3(left)
        yh, ym, yl = split3(y)
        a = jnp.concatenate([lh, lh, lm, lh, ll, lm], axis=0).astype(BF)
        b = jnp.concatenate([yh, ym, yh, yl, yh, ym], axis=0).astype(BF)
        upd = dot_f32(a, b, ((0,), (0,)))
        new = jnp.where(col < 8, 0.0, x) - upd
        new = jnp.where(row < K - 8 * k, new, x)
        return pltpu.roll(jnp.concatenate([new[8:, :], y], axis=0), K - 8, axis=1)

    x = lax.fori_loop(0, K // 8, step, gram)
    return jnp.where(col <= row, x, 0.0)


def kernel(
    tile,
    start,
    basis_out,
    second_out,
    thi,
    tlo,
    thit,
    tlot,
    right,
    rwide,
    left,
    lpart,
    lcore,
    lx,
    ly,
    lsum,
    wpart,
    wz,
    gram1,
    g1z,
    g1share,
    gram2,
    g2core,
    g2x,
    g2y,
    g2sum,
    factor,
    send,
    recv,
):
    d = lax.axis_index("dp")
    z = lax.axis_index("row")
    c = lax.axis_index("col")
    co = lax.rem(c, 2)
    yl = lax.rem(lax.div(c, 2), 2)
    x = lax.div(c, 4)
    y = d * 2 + yl

    def dev_core():
        return (d, z, c + 1 - 2 * co)

    def dev_x(i):
        return (d, z, i * 4 + yl * 2 + co)

    def dev_y(i):
        return (lax.div(i, 2), z, x * 4 + lax.rem(i, 2) * 2 + co)

    def dev_z(i):
        return (d, i, c)

    barrier = pltpu.get_barrier_semaphore()
    peers = [dev_core()]
    peers += [dev_x(lax.rem(x + o, 4)) for o in (1, 3, 2)]
    peers += [dev_y(lax.rem(y + o, 4)) for o in (1, 3, 2)]
    peers += [dev_z(lax.rem(z + o, 8)) for o in (1, 7, 2, 6, 3, 5, 4)]
    for dev in peers:
        pl.semaphore_signal(barrier, inc=1, device_id=dev, device_id_type=MESH)

    for i in range(TR // 128):
        part = tile[i * 128 : (i + 1) * 128, :]
        hi, lo = split2(part)
        thi[i * 128 : (i + 1) * 128, :] = hi
        tlo[i * 128 : (i + 1) * 128, :] = lo
        hi, lo = split2(part.T)
        thit[:, i * 128 : (i + 1) * 128] = hi
        tlot[:, i * 128 : (i + 1) * 128] = lo
    right[...] = start[...] * math.sqrt(3.0 / N)
    rwide[...] = wide(right[...])
    pl.semaphore_wait(barrier, len(peers))

    def copy(src, dst, it, slot_out, slot_in, dev):
        return pltpu.make_async_remote_copy(
            src_ref=src,
            dst_ref=dst,
            send_sem=send.at[it, slot_out],
            recv_sem=recv.at[it, slot_in],
            device_id=dev,
            device_id_type=MESH,
        )

    def ring(n, me, dev, base, it, src, dst):
        for o in sorted(range(1, n), key=lambda o: min(o, n - o)):
            i = lax.rem(me + o, n)
            copy(src(i), dst(me), it, base + o, base + o, dev(i)).start()

    def ring_wait(n, me, dev, base, it, src, dst):
        for o in sorted(range(1, n), key=lambda o: min(o, n - o)):
            i = lax.rem(me + n - o, n)
            copy(src(i), dst(i), it, base + o, base + o, dev(i)).wait()

    def blocks(ref, size):
        return lambda i: ref.at[pl.ds(pl.multiple_of(i * size, size), size), :]

    class Plane:
        def __init__(self, it, rows, part, core_buf, x_buf, y_buf, total, sems):
            self.it, self.rows = it, rows
            self.part, self.core_buf, self.x_buf, self.y_buf, self.total = part, core_buf, x_buf, y_buf, total
            self.s_core, self.s_x, self.s_y, self.s_xg, self.s_cg = sems
            self.half, self.unit = rows // 2, rows // 8

        def mine(self):
            return pl.ds(pl.multiple_of(co * self.half + x * self.unit, self.unit), self.unit)

        def core_copy(self):
            there = pl.ds(pl.multiple_of((1 - co) * self.half, self.half), self.half)
            return copy(self.part.at[there, :], self.core_buf.at[self.it], self.it, self.s_core, self.s_core, dev_core())

        def core_done(self):
            self.core_copy().wait()
            here = pl.ds(pl.multiple_of(co * self.half, self.half), self.half)
            self.core_buf[self.it] = self.core_buf[self.it] + self.part[here, :]

        def x_args(self):
            src = lambda i: self.core_buf.at[self.it, pl.ds(pl.multiple_of(i * self.unit, self.unit), self.unit), :]
            return (4, x, dev_x, self.s_x, self.it, src, lambda i: self.x_buf.at[self.it, i])

        def x_send(self):
            own = self.core_buf[self.it, pl.ds(pl.multiple_of(x * self.unit, self.unit), self.unit), :]
            self.x_buf[self.it, x] = own
            ring(*self.x_args())

        def x_done(self):
            ring_wait(*self.x_args())
            self.y_buf[self.it, y] = (self.x_buf[self.it, 0] + self.x_buf[self.it, 1]) + (
                self.x_buf[self.it, 2] + self.x_buf[self.it, 3]
            )

        def y_args(self):
            return (
                4,
                y,
                dev_y,
                self.s_y,
                self.it,
                lambda i: self.y_buf.at[self.it, y],
                lambda i: self.y_buf.at[self.it, i],
            )

        def y_send(self):
            ring(*self.y_args())

        def y_done(self):
            ring_wait(*self.y_args())
            self.total[self.mine(), :] = (self.y_buf[self.it, 0] + self.y_buf[self.it, 1]) + (
                self.y_buf[self.it, 2] + self.y_buf[self.it, 3]
            )

        def xg_args(self):
            place = lambda i: self.total.at[pl.ds(pl.multiple_of(co * self.half + i * self.unit, self.unit), self.unit), :]
            return (4, x, dev_x, self.s_xg, self.it, lambda i: place(x), place)

        def xg_send(self):
            ring(*self.xg_args())

        def xg_done(self):
            ring_wait(*self.xg_args())

        def cg_copy(self):
            here = self.total.at[pl.ds(pl.multiple_of(co * self.half, self.half), self.half), :]
            return copy(here, here, self.it, self.s_cg, self.s_cg, dev_core())

    def left_plane(it):
        return Plane(it, TR, lpart, lcore, lx, ly, lsum, (L_CORE, L_X, L_Y, L_XG, L_CG))

    def second_plane(it):
        return Plane(it, K, gram2, g2core, g2x, g2y, g2sum, (G2_CORE, G2_X, G2_Y, G2_XG, G2_CG))

    def iteration(it, carry):
        lp, sp = left_plane(it), second_plane(it)

        @pl.when(it > 0)
        def _():
            gram2[...] = full_dot(right[...], right[...], ((0,), (0,)))
            sp.core_copy().start()

        lpart[...] = split_product(thi[...], tlo[...], rwide[...])
        lp.core_copy().start()

        @pl.when(it > 0)
        def _():
            sp.core_done()
            sp.x_send()

        lp.core_done()
        lp.x_send()

        @pl.when(it > 0)
        def _():
            sp.x_done()
            sp.y_send()

        lp.x_done()
        lp.y_send()

        @pl.when(it > 0)
        def _():
            sp.y_done()
            sp.xg_send()

        lp.y_done()
        lp.xg_send()

        @pl.when(it > 0)
        def _():
            sp.xg_done()
            sp.cg_copy().start()

        lp.xg_done()
        lp.cg_copy().start()

        @pl.when(it > 0)
        def _():
            sp.cg_copy().wait()
            factor[...] = inverse_factor(g2sum[...])

        lp.cg_copy().wait()

        @pl.when(it == 0)
        def _():
            left[...] = lsum[...]

        @pl.when(it > 0)
        def _():
            left[...] = full_dot(lsum[...], factor[...], ((1,), (1,)))

        gram1[...] = full_dot(left[...], left[...], ((0,), (0,)))
        g1_rs = (8, z, dev_z, G1_RS, it, blocks(gram1, 16), lambda i: g1z.at[it, i])
        g1z[it, z] = gram1[pl.ds(pl.multiple_of(z * 16, 16), 16), :]
        ring(*g1_rs)

        lwide = wide(left[...])
        wpart[...] = split_product(thit[...], tlot[...], lwide)
        w_rs = (8, z, dev_z, W_RS, it, blocks(wpart, ZB), lambda i: wz.at[it, i])
        wz[it, z] = wpart[pl.ds(pl.multiple_of(z * ZB, 16), ZB), :]
        ring(*w_rs)

        ring_wait(*g1_rs)
        total = g1z[it, 0]
        for i in range(1, 8):
            total = total + g1z[it, i]
        g1share[pl.ds(pl.multiple_of(z * 16, 16), 16), :] = total
        share = blocks(g1share, 16)
        g1_ag = (8, z, dev_z, G1_AG, it, lambda i: share(z), share)
        ring(*g1_ag)

        ring_wait(*w_rs)
        total = wz[it, 0]
        for i in range(1, 8):
            total = total + wz[it, i]
        right[pl.ds(pl.multiple_of(z * ZB, 16), ZB), :] = total
        place = blocks(right, ZB)
        w_ag = (8, z, dev_z, W_AG, it, lambda i: place(z), place)
        ring(*w_ag)

        ring_wait(*g1_ag)
        factor[...] = inverse_factor(g1share[...])
        ring_wait(*w_ag)
        right[...] = full_dot(right[...], factor[...], ((1,), (1,)))
        rwide[...] = wide(right[...])
        return carry

    lax.fori_loop(0, ITERS, iteration, 0)

    sp = second_plane(ITERS)
    gram2[...] = full_dot(right[...], right[...], ((0,), (0,)))
    sp.core_copy().start()
    sp.core_done()
    sp.x_send()
    sp.x_done()
    sp.y_send()
    sp.y_done()
    sp.xg_send()
    sp.xg_done()
    sp.cg_copy().start()
    sp.cg_copy().wait()
    second_out[...] = g2sum[...]
    basis_out[...] = full_dot(right[...], inverse_factor(g2sum[...]), ((1,), (1,)))


def power(tile, start):
    vm = lambda *shape: pltpu.VMEM(shape, F32)
    its = ITERS + 1
    return pl.pallas_call(
        kernel,
        out_shape=(jax.ShapeDtypeStruct((TC, K), F32), jax.ShapeDtypeStruct((K, K), F32)),
        in_specs=[pl.BlockSpec(memory_space=pltpu.VMEM)] * 2,
        out_specs=[pl.BlockSpec(memory_space=pltpu.VMEM)] * 2,
        scratch_shapes=[
            pltpu.VMEM((TR, TC), BF),
            pltpu.VMEM((TR, TC), BF),
            pltpu.VMEM((TC, TR), BF),
            pltpu.VMEM((TC, TR), BF),
            vm(TC, K),
            pltpu.VMEM((TC, 2 * K), BF),
            vm(TR, K),
            vm(TR, K),
            vm(its, TR // 2, K),
            vm(its, 4, TR // 8, K),
            vm(its, 4, TR // 8, K),
            vm(TR, K),
            vm(TC, K),
            vm(its, 8, ZB, K),
            vm(K, K),
            vm(its, 8, 16, K),
            vm(K, K),
            vm(K, K),
            vm(its, K // 2, K),
            vm(its, 4, K // 8, K),
            vm(its, 4, K // 8, K),
            vm(K, K),
            vm(K, K),
            pltpu.SemaphoreType.DMA((its, SEMS)),
            pltpu.SemaphoreType.DMA((its, SEMS)),
        ],
        compiler_params=pltpu.CompilerParams(
            collective_id=0, has_side_effects=True, vmem_limit_bytes=56 * 2**20
        ),
        name="power",
    )(tile, start)


def body(partials, clip_ratio, start_block):
    summed = lax.psum_scatter(partials[0], "dp", scatter_dimension=1, tiled=True)
    tile = lax.all_to_all(summed, "col", split_axis=1, concat_axis=0, tiled=True)
    vectors, second = power(tile, start_block)
    sigma = jnp.sqrt(jnp.sqrt(jnp.sum(second * second)))
    limit = clip_ratio[0] * (math.sqrt(M) + math.sqrt(N))
    scale = limit / sigma
    update = summed * scale
    return (update, vectors)


def solution(mesh):
    placed = (P("dp", ("row", "col"), None), P(), P(("dp", "col"), None))
    return jax.shard_map(
        body,
        mesh=mesh,
        in_specs=placed,
        out_specs=(P(("row", "col"), "dp"), P(("dp", "col"), None)),
        check_vma=False,
    )
```

time: 1470 us -> 414 us (0.28)
  waiting for transfers between devices: 1180 us -> 148 us
  Pallas kernels: 0 us -> 235 us
  other arithmetic: 148 us -> 5.69 us
  matrix products: 57.4 us -> 0 us
  blocking collectives: 48.2 us -> 0 us
    psum x12 -> x0, waiting for transfers between devices: 1080 us -> none  [the longest x3 337 us: body(): left = lax.psum(times_tile(tile, vectors), ('dp', 'col'))]
    pallas_call x0 -> x1, Pallas kernels: none -> 235 us  [power(): pl.pallas_call(kernel, out_shape=(jax.ShapeDtypeStruct((TC, K), F32), jax...]
    another operation x30 -> x0, other arithmetic: 137 us -> none  [the longest x18 74.3 us: orthonormal(): factor = jnp.linalg.cholesky(gram)]
    all_to_all x1 -> x0, blocking collectives: 48.2 us -> none  [body(): lax.all_to_all(summed, 'col', split_axis=1, concat_axis=0, tiled=True)]
    dot_general x12 -> x0, matrix products: 47.7 us -> none  [the longest x3 18.1 us: times_tile(): jnp.dot(tile, block, precision=lax.Precision.HIGHEST, preferred_element_t...]
    all_to_all x0 -> x1, waiting for transfers between devices: none -> 45.4 us  [body(): lax.all_to_all(summed, 'col', split_axis=1, concat_axis=0, tiled=True)]
  transfers between devices with their start and end apart: 13 -> 2, of which waited for: 13 -> 2; matrix products, arithmetic and copies ran while one was open for 0% -> 0% of each run, Pallas kernels for 0% -> 0%
where the time goes in v1:
time: 414 us
  Pallas kernels  235 us (57%)
  waiting for transfers between devices  148 us (36%)
  between operations  15.4 us (4%)
  other arithmetic  5.69 us (1%)
  local copies, waits for them, and re-layouts  5.03 us (1%)
  starting transfers between devices  4.99 us (1%)
    pallas_call x1, Pallas kernels, power(): pl.pallas_call(kernel, out_shape=(jax.ShapeDtypeStruct((TC, K), F32), jax...  235 us
    reduce_scatter x1, waiting for transfers between devices, body(): lax.psum_scatter(partials[0], 'dp', scatter_dimension=1, tiled=True)  102 us
    all_to_all x1, waiting for transfers between devices, body(): lax.all_to_all(summed, 'col', split_axis=1, concat_axis=0, tiled=True)  45.4 us
  transfers between devices with their start and end apart: 2, of which 2 were waited for; matrix products, arithmetic and copies ran while one was open for 0% of the time, Pallas kernels for 0%

profile of v1, /device:TPU:1, one launch (start us, length us, event | category | flops | bytes accessed | tf_op | source)
XLA Modules:
  0.0 413.9 jit_solution(5411317653194338544)
XLA Ops:
  7.2 0.0 reduce-scatter.2.cloned.1.call-start
  7.2 0.7 reduce-scatter.2.cloned.1.call-update
  7.9 101.5 %reduce-scatter.2.cloned.1.call-done = f32[64,14336]{1,0:T(8,128)} async-done(((f32[64,28672]{1,0:T(8,128)}), f32[64,14336]{1,0:T(8,128)}) %reduce-scatter.2.cloned.1.call-update) | async-done | bytes 3670032 | tf_op jit(solution)/shard_map/reduce_scatter | solution.py:414
  109.4 4.3 %copy.8 = f32[8,16,8,896]{3,2,0,1:T(8,128)} copy(f32[8,16,8,896]{3,2,1,0:T(8,128)} %bitcast.10) | data formatting | bytes 7340032 | tf_op jit(solution)/shard_map/all_to_all | solution.py:415
  113.7 5.0 %all-to-all-start = ((f32[64,16,896]{2,0,1:T(8,128)}), f32[64,16,896]{2,0,1:T(8,128)}, u32[]{:S(2)}, u32[]{:S(2)}) async-start(f32[64,16,896]{2,0,1:T(8,128)} %bitcast.9), calls=%async_computation.1 | async-start | bytes 7340032 | tf_op jit(solution)/shard_map/all_to_all | solution.py:415
  119.3 45.4 %all-to-all-done = f32[64,16,896]{2,0,1:T(8,128)} async-done(((f32[64,16,896]{2,0,1:T(8,128)}), f32[64,16,896]{2,0,1:T(8,128)}, u32[]{:S(2)}, u32[]{:S(2)}) %all-to-all-start) | async-done | bytes 3670048 | tf_op jit(solution)/shard_map/all_to_all | solution.py:415
  164.7 235.1 %power.1 = (f32[896,128]{1,0:T(8,128)}, f32[128,128]{1,0:T(8,128)}) custom-call(f32[1024,896]{1,0:T(8,128)} %bitcast.3.tile, f32[896,128]{1,0:T(8,128)} %start.1), custom_call_target="tpu_custom_call" | custom-call | tf_op jit(solution)/shard_map/power/pallas_call | solution.py:374
  399.8 1.5 multiply_reduce_fusion
  402.0 0.0 copy-start
  402.0 4.2 %broadcast_multiply_fusion = f32[64,14336]{1,0:T(8,128)} fusion(f32[64,14336]{1,0:T(8,128)} %reduce-scatter.2.cloned.1.call-done, f32[]{:T(128)S(6)} %div.3), kind=kLoop, calls=%fused_computation.1 | loop fusion | flops 917504 | bytes 7340036 | tf_op jit(solution)/shard_map/mul | solution.py:420
  406.2 0.0 copy-done
  406.3 0.8 copy.11
Async XLA Ops:
  7.2 102.3 %reduce-scatter.2.cloned.1.call-start = ((), (), s32[]{:S(2)}) async-start(), calls=%async_computation.2 | async-start | bytes 11010048 | tf_op jit(solution)/shard_map/reduce_scatter | solution.py:414
  113.7 51.0 %all-to-all-start = ((f32[64,16,896]{2,0,1:T(8,128)}), f32[64,16,896]{2,0,1:T(8,128)}, u32[]{:S(2)}, u32[]{:S(2)}) async-start(f32[64,16,896]{2,0,1:T(8,128)} %bitcast.9), calls=%async_computation.1 | async-start | bytes 7340032 | tf_op jit(solution)/shard_map/all_to_all | solution.py:415
  402.0 4.2 %copy-start = (f32[896,128]{1,0:T(8,128)S(1)}, f32[896,128]{1,0:T(8,128)}, u32[]{:S(2)}) copy-start(f32[896,128]{1,0:T(8,128)} %get-tuple-element.9) | copy-start | bytes 1376260
Sparse Core Ops, SparseCore 0:
  10.6 98.8 reduce-scatter.1

commit v2 on v1

--- a/solution.py
+++ b/solution.py
@@ -13,6 +13,10 @@
 ITERS = 3
 TR = 1024
 TC = 896
+ROWS = 64
+HALF = N // 2
+CHUNKS = 8
+WINDOW = 2
 ZB = 112
 MESH = pl.DeviceIdType.MESH
 BF = jnp.bfloat16
@@ -89,10 +93,24 @@
 
 
 def kernel(
-    tile,
+    partial,
     start,
     basis_out,
     second_out,
+    summed_out,
+    own,
+    theirs,
+    summed,
+    tile,
+    dp_send,
+    dp_recv,
+    own_sem,
+    out_sem,
+    tile_send,
+    tile_recv,
+    start_sem,
+    end_sem,
+    moved,
     thi,
     tlo,
     thit,
@@ -125,7 +143,11 @@
     co = lax.rem(c, 2)
     yl = lax.rem(lax.div(c, 2), 2)
     x = lax.div(c, 4)
-    y = d * 2 + yl
+    zl = lax.rem(z, 2)
+    zh = lax.div(z, 2)
+    y = d * 2 + zl
+    p = yl * 4 + zh
+    j = x * 4 + zl * 2 + co
 
     def dev_core():
         return (d, z, c + 1 - 2 * co)
@@ -134,30 +156,132 @@
         return (d, z, i * 4 + yl * 2 + co)
 
     def dev_y(i):
-        return (lax.div(i, 2), z, x * 4 + lax.rem(i, 2) * 2 + co)
-
-    def dev_z(i):
-        return (d, i, c)
+        return (lax.div(i, 2), zh * 2 + lax.rem(i, 2), c)
+
+    def dev_p(i):
+        return (d, lax.rem(i, 4) * 2 + zl, x * 4 + lax.div(i, 4) * 2 + co)
+
+    def dev_j(i):
+        return (d, zh * 2 + lax.rem(lax.div(i, 2), 2), lax.div(i, 4) * 4 + yl * 2 + lax.rem(i, 2))
+
+    partner = (1 - d, z, c)
+    across = (d, z, x * 4 + (1 - yl) * 2 + co)
+    above = (d, lax.rem(z + 1, 8), c)
+    below = (d, lax.rem(z + 7, 8), c)
 
     barrier = pltpu.get_barrier_semaphore()
-    peers = [dev_core()]
-    peers += [dev_x(lax.rem(x + o, 4)) for o in (1, 3, 2)]
+    peers = [partner, across, above, below]
     peers += [dev_y(lax.rem(y + o, 4)) for o in (1, 3, 2)]
-    peers += [dev_z(lax.rem(z + o, 8)) for o in (1, 7, 2, 6, 3, 5, 4)]
+    peers += [dev_p(lax.rem(p + o, 8)) for o in (1, 7, 2, 6, 3, 5, 4)]
+    peers += [dev_j(lax.rem(j + o, 16)) for o in range(1, 16)]
     for dev in peers:
         pl.semaphore_signal(barrier, inc=1, device_id=dev, device_id_type=MESH)
 
-    for i in range(TR // 128):
-        part = tile[i * 128 : (i + 1) * 128, :]
+    def own_copy(k):
+        rows = pl.ds(pl.multiple_of(k * 8, 8), 8)
+        mine = pl.ds(pl.multiple_of(d * HALF, HALF), HALF)
+        return pltpu.make_async_copy(partial.at[rows, mine], own.at[rows, :], own_sem.at[k])
+
+    def dp_copy(k):
+        rows = pl.ds(pl.multiple_of(k * 8, 8), 8)
+        other = pl.ds(pl.multiple_of((1 - d) * HALF, HALF), HALF)
+        return pltpu.make_async_remote_copy(
+            src_ref=partial.at[rows, other],
+            dst_ref=theirs.at[rows, :],
+            send_sem=dp_send.at[k],
+            recv_sem=dp_recv.at[k],
+            device_id=partner,
+            device_id_type=MESH,
+        )
+
+    start_here = pltpu.make_async_copy(start, right, start_sem.at[0])
+    start_across = pltpu.make_async_remote_copy(
+        src_ref=start,
+        dst_ref=right,
+        send_sem=start_sem.at[1],
+        recv_sem=start_sem.at[2],
+        device_id=across,
+        device_id_type=MESH,
+    )
+
+    for k in range(CHUNKS):
+        own_copy(k).start()
+    pl.semaphore_wait(barrier, len(peers))
+    for k in range(WINDOW):
+        dp_copy(k).start()
+
+    @pl.when(yl == zl)
+    def _():
+        start_here.start()
+
+    def prepare(k):
+        rows = pl.ds(pl.multiple_of(k * 128, 128), 128)
+        got = tile.at[pl.ds(0, 120), :]
+        pltpu.make_async_copy(got, got, tile_recv.at[k]).wait()
+        part = tile[rows, :]
         hi, lo = split2(part)
-        thi[i * 128 : (i + 1) * 128, :] = hi
-        tlo[i * 128 : (i + 1) * 128, :] = lo
+        thi[rows, :] = hi
+        tlo[rows, :] = lo
         hi, lo = split2(part.T)
-        thit[:, i * 128 : (i + 1) * 128] = hi
-        tlot[:, i * 128 : (i + 1) * 128] = lo
-    right[...] = start[...] * math.sqrt(3.0 / N)
+        thit[:, rows] = hi
+        tlot[:, rows] = lo
+
+    def chunk(k, carry):
+        rows = pl.ds(pl.multiple_of(k * 8, 8), 8)
+        place = pl.ds(pl.multiple_of(k * 128 + j * 8, 8), 8)
+        dp_copy(k).wait()
+
+        @pl.when(k + WINDOW < CHUNKS)
+        def _():
+            dp_copy(k + WINDOW).start()
+
+        @pl.when((k == CHUNKS - 1) & (yl == zl))
+        def _():
+            start_across.start()
+
+        own_copy(k).wait()
+        summed[rows, :] = own[rows, :] + theirs[rows, :]
+
+        def block(i):
+            return summed.at[rows, pl.ds(pl.multiple_of(i * TC, 128), TC)]
+
+        for o in range(1, 16):
+            i = lax.rem(j + o, 16)
+            pltpu.make_async_remote_copy(
+                src_ref=block(i),
+                dst_ref=tile.at[place, :],
+                send_sem=tile_send.at[k],
+                recv_sem=tile_recv.at[k],
+                device_id=dev_j(i),
+                device_id_type=MESH,
+            ).start()
+        tile[place, :] = block(j)[...]
+
+        @pl.when(k > 0)
+        def _():
+            prepare(k - 1)
+
+        return carry
+
+    lax.fori_loop(0, CHUNKS, chunk, 0)
+    out_copy = pltpu.make_async_copy(summed, summed_out, out_sem)
+    out_copy.start()
+    prepare(CHUNKS - 1)
+    for k in range(CHUNKS):
+        sent = tile.at[pl.ds(0, 120), :]
+        pltpu.make_async_copy(sent, sent, tile_send.at[k]).wait()
+
+    @pl.when(yl == zl)
+    def _():
+        start_here.wait()
+        start_across.wait_send()
+
+    @pl.when(yl != zl)
+    def _():
+        start_across.wait_recv()
+
+    right[...] = right[...] * math.sqrt(3.0 / N)
     rwide[...] = wide(right[...])
-    pl.semaphore_wait(barrier, len(peers))
 
     def copy(src, dst, it, slot_out, slot_in, dev):
         return pltpu.make_async_remote_copy(
@@ -315,32 +439,32 @@
             left[...] = full_dot(lsum[...], factor[...], ((1,), (1,)))
 
         gram1[...] = full_dot(left[...], left[...], ((0,), (0,)))
-        g1_rs = (8, z, dev_z, G1_RS, it, blocks(gram1, 16), lambda i: g1z.at[it, i])
-        g1z[it, z] = gram1[pl.ds(pl.multiple_of(z * 16, 16), 16), :]
+        g1_rs = (8, p, dev_p, G1_RS, it, blocks(gram1, 16), lambda i: g1z.at[it, i])
+        g1z[it, p] = gram1[pl.ds(pl.multiple_of(p * 16, 16), 16), :]
         ring(*g1_rs)
 
         lwide = wide(left[...])
         wpart[...] = split_product(thit[...], tlot[...], lwide)
-        w_rs = (8, z, dev_z, W_RS, it, blocks(wpart, ZB), lambda i: wz.at[it, i])
-        wz[it, z] = wpart[pl.ds(pl.multiple_of(z * ZB, 16), ZB), :]
+        w_rs = (8, p, dev_p, W_RS, it, blocks(wpart, ZB), lambda i: wz.at[it, i])
+        wz[it, p] = wpart[pl.ds(pl.multiple_of(p * ZB, 16), ZB), :]
         ring(*w_rs)
 
         ring_wait(*g1_rs)
         total = g1z[it, 0]
         for i in range(1, 8):
             total = total + g1z[it, i]
-        g1share[pl.ds(pl.multiple_of(z * 16, 16), 16), :] = total
+        g1share[pl.ds(pl.multiple_of(p * 16, 16), 16), :] = total
         share = blocks(g1share, 16)
-        g1_ag = (8, z, dev_z, G1_AG, it, lambda i: share(z), share)
+        g1_ag = (8, p, dev_p, G1_AG, it, lambda i: share(p), share)
         ring(*g1_ag)
 
         ring_wait(*w_rs)
         total = wz[it, 0]
         for i in range(1, 8):
             total = total + wz[it, i]
-        right[pl.ds(pl.multiple_of(z * ZB, 16), ZB), :] = total
+        right[pl.ds(pl.multiple_of(p * ZB, 16), ZB), :] = total
         place = blocks(right, ZB)
-        w_ag = (8, z, dev_z, W_AG, it, lambda i: place(z), place)
+        w_ag = (8, p, dev_p, W_AG, it, lambda i: place(p), place)
         ring(*w_ag)
 
         ring_wait(*g1_ag)
@@ -365,18 +489,64 @@
     sp.cg_copy().start()
     sp.cg_copy().wait()
     second_out[...] = g2sum[...]
-    basis_out[...] = full_dot(right[...], inverse_factor(g2sum[...]), ((1,), (1,)))
-
-
-def power(tile, start):
+    right[...] = full_dot(right[...], inverse_factor(g2sum[...]), ((1,), (1,)))
+
+    def end_copy(i, dev):
+        rows = pl.ds(i * (TC // 2), TC // 2)
+        return pltpu.make_async_remote_copy(
+            src_ref=right.at[rows, :],
+            dst_ref=moved.at[rows, :],
+            send_sem=end_sem.at[i],
+            recv_sem=end_sem.at[2 + i],
+            device_id=dev,
+            device_id_type=MESH,
+        )
+
+    ends = [end_copy(0, above), end_copy(1, below)]
+
+    @pl.when(yl == zl)
+    def _():
+        for e in ends:
+            e.start()
+        basis_out[...] = right[...]
+        for e in ends:
+            e.wait_send()
+
+    @pl.when(yl != zl)
+    def _():
+        for e in ends:
+            e.wait_recv()
+        basis_out[...] = moved[...]
+
+    out_copy.wait()
+
+
+def power(partial, start):
     vm = lambda *shape: pltpu.VMEM(shape, F32)
     its = ITERS + 1
     return pl.pallas_call(
         kernel,
-        out_shape=(jax.ShapeDtypeStruct((TC, K), F32), jax.ShapeDtypeStruct((K, K), F32)),
-        in_specs=[pl.BlockSpec(memory_space=pltpu.VMEM)] * 2,
-        out_specs=[pl.BlockSpec(memory_space=pltpu.VMEM)] * 2,
+        out_shape=(
+            jax.ShapeDtypeStruct((TC, K), F32),
+            jax.ShapeDtypeStruct((K, K), F32),
+            jax.ShapeDtypeStruct((ROWS, HALF), F32),
+        ),
+        in_specs=[pl.BlockSpec(memory_space=pl.ANY)] * 2,
+        out_specs=[pl.BlockSpec(memory_space=pltpu.VMEM)] * 2 + [pl.BlockSpec(memory_space=pl.ANY)],
         scratch_shapes=[
+            vm(ROWS, HALF),
+            vm(ROWS, HALF),
+            vm(ROWS, HALF),
+            vm(TR, TC),
+            pltpu.SemaphoreType.DMA((CHUNKS,)),
+            pltpu.SemaphoreType.DMA((CHUNKS,)),
+            pltpu.SemaphoreType.DMA((CHUNKS,)),
+            pltpu.SemaphoreType.DMA,
+            pltpu.SemaphoreType.DMA((CHUNKS,)),
+            pltpu.SemaphoreType.DMA((CHUNKS,)),
+            pltpu.SemaphoreType.DMA((3,)),
+            pltpu.SemaphoreType.DMA((4,)),
+            vm(TC, K),
             pltpu.VMEM((TR, TC), BF),
             pltpu.VMEM((TR, TC), BF),
             pltpu.VMEM((TC, TR), BF),
@@ -404,16 +574,14 @@
             pltpu.SemaphoreType.DMA((its, SEMS)),
         ],
         compiler_params=pltpu.CompilerParams(
-            collective_id=0, has_side_effects=True, vmem_limit_bytes=56 * 2**20
+            collective_id=0, has_side_effects=True, vmem_limit_bytes=60 * 2**20
         ),
         name="power",
-    )(tile, start)
+    )(partial, start)
 
 
 def body(partials, clip_ratio, start_block):
-    summed = lax.psum_scatter(partials[0], "dp", scatter_dimension=1, tiled=True)
-    tile = lax.all_to_all(summed, "col", split_axis=1, concat_axis=0, tiled=True)
-    vectors, second = power(tile, start_block)
+    vectors, second, summed = power(partials[0], start_block)
     sigma = jnp.sqrt(jnp.sqrt(jnp.sum(second * second)))
     limit = clip_ratio[0] * (math.sqrt(M) + math.sqrt(N))
     scale = limit / sigma

time: 414 us -> 349 us (0.84)
  waiting for transfers between devices: 148 us -> 0 us
  Pallas kernels: 235 us -> 336 us
  between operations: 15.4 us -> 2.03 us
  starting transfers between devices: 4.99 us -> 0 us
  local copies, waits for them, and re-layouts: 5.03 us -> 0.77 us
    reduce_scatter x1 -> x0, waiting for transfers between devices: 102 us -> none  [body(): lax.psum_scatter(partials[0], 'dp', scatter_dimension=1, tiled=True)]
    pallas_call x1, Pallas kernels: 235 us -> 336 us  [power(): pl.pallas_call(kernel, out_shape=(jax.ShapeDtypeStruct((TC, K), F32), jax...]
    all_to_all x1 -> x0, waiting for transfers between devices: 45.4 us -> none  [body(): lax.all_to_all(summed, 'col', split_axis=1, concat_axis=0, tiled=True)]
    all_to_all x1 -> x0, starting transfers between devices: 4.95 us -> none  [body(): lax.all_to_all(summed, 'col', split_axis=1, concat_axis=0, tiled=True)]
    all_to_all x1 -> x0, local copies, waits for them, and re-layouts: 4.26 us -> none  [body(): lax.all_to_all(summed, 'col', split_axis=1, concat_axis=0, tiled=True)]
  transfers between devices with their start and end apart: 2 -> 0, of which waited for: 2 -> 0; matrix products, arithmetic and copies ran while one was open for 0% -> 0% of each run, Pallas kernels for 0% -> 0%
where the time goes in v2:
time: 349 us; the launch traced here: 345 us
  Pallas kernels  336 us (96%)
  other arithmetic  5.69 us (2%)
    pallas_call x1, Pallas kernels, power(): pl.pallas_call(kernel, out_shape=(jax.ShapeDtypeStruct((TC, K), F32), jax...  336 us

profile of v2, /device:TPU:1, one launch (start us, length us, event | category | flops | bytes accessed | tf_op | source)
XLA Modules:
  0.0 344.9 jit_solution(14485617286382338442)
XLA Ops:
  1.3 336.4 %power.1 = (f32[896,128]{1,0:T(8,128)}, f32[128,128]{1,0:T(8,128)}, f32[64,14336]{1,0:T(8,128)}) custom-call(f32[64,28672]{1,0:T(8,128)} %bitcast.2, f32[896,128]{1,0:T(8,128)} %start.1), custom_call_target="tpu_custom_call" | custom-call | tf_op jit(solution)/shard_map/power/pallas_call | solution.py:527
  337.7 1.5 multiply_reduce_fusion
  339.9 0.0 copy-start
  339.9 4.2 %broadcast_multiply_fusion = f32[64,14336]{1,0:T(8,128)} fusion(f32[64,14336]{1,0:T(8,128)} %get-tuple-element.5, f32[]{:T(128)S(6)} %div.3), kind=kLoop, calls=%fused_computation | loop fusion | flops 917504 | bytes 7340036 | tf_op jit(solution)/shard_map/mul | solution.py:588
  344.1 0.0 copy-done
  344.1 0.8 copy.7
Async XLA Ops:
  339.9 4.2 %copy-start = (f32[896,128]{1,0:T(8,128)S(1)}, f32[896,128]{1,0:T(8,128)}, u32[]{:S(2)}) copy-start(f32[896,128]{1,0:T(8,128)} %get-tuple-element.11) | copy-start | bytes 1376260

commit v3 on v2

--- a/solution.py
+++ b/solution.py
@@ -16,16 +16,17 @@
 ROWS = 64
 HALF = N // 2
 CHUNKS = 8
+PANEL = 16
 WINDOW = 2
 ZB = 112
 MESH = pl.DeviceIdType.MESH
 BF = jnp.bfloat16
 F32 = jnp.float32
 
-G2_CORE, G2_X, G2_Y, G2_XG, G2_CG = 0, 1, 5, 9, 13
-L_CORE, L_X, L_Y, L_XG, L_CG = 14, 15, 19, 23, 27
-G1_RS, G1_AG, W_RS, W_AG = 28, 36, 44, 52
-SEMS = 60
+G2_CORE, G2_X, G2_Y, G2_CG = 0, 1, 5, 9
+L_CORE, L_X, L_Y, L_XG, L_CG = 10, 11, 15, 19, 23
+G1_RS, G1_AG, G1_CG, W_RS, W_AG = 24, 32, 40, 41, 49
+SEMS = 57
 
 
 def split2(a):
@@ -54,49 +55,52 @@
 
 
 def inverse_factor(gram):
-    lane = lax.broadcasted_iota(jnp.int32, (8, K), 1)
-    sub = lax.broadcasted_iota(jnp.int32, (8, K), 0)
+    lane = lax.broadcasted_iota(jnp.int32, (PANEL, K), 1)
+    sub = lax.broadcasted_iota(jnp.int32, (PANEL, K), 0)
     col = lax.broadcasted_iota(jnp.int32, (K, K), 1)
     row = lax.broadcasted_iota(jnp.int32, (K, K), 0)
 
+    def split3(a):
+        hi = a.astype(BF).astype(F32)
+        mid = (a - hi).astype(BF).astype(F32)
+        return hi, mid, a - hi - mid
+
     def step(k, x):
-        p = x[0:8, :]
-        q = jnp.where(lane == sub, 1.0, 0.0).astype(F32)
-        for j in range(8):
-            piv = p[j : j + 1, j : j + 1]
-            rs = lax.rsqrt(piv)
-            rs = rs * (1.5 - 0.5 * piv * rs * rs)
-            urow = p[j : j + 1, :] * rs
-            qrow = q[j : j + 1, :] * rs
-            m = jnp.where(sub > j, p[:, j : j + 1] * rs, 0.0)
-            p = jnp.where(sub == j, urow, p - m * urow)
-            q = jnp.where(sub == j, qrow, q - m * qrow)
-        y = jnp.where(lane < 8, q, p)
-        left = jnp.where((lane >= 8) & (lane < K - 8 * k), p, 0.0)
-
-        def split3(a):
-            hi = a.astype(BF).astype(F32)
-            mid = (a - hi).astype(BF).astype(F32)
-            return hi, mid, a - hi - mid
-
-        lh, lm, ll = split3(left)
+        p = x[0:PANEL, :]
+        cols = [jnp.broadcast_to(p[:, i : i + 1], (PANEL, K)) for i in range(PANEL)]
+        pivots = []
+        for j in range(PANEL):
+            heads = [cols[i][j : j + 1, :] for i in range(j, PANEL)]
+            pivots.append(heads[0])
+            m = jnp.where(sub > j, cols[j] * (1.0 / heads[0]), 0.0)
+            for i in range(j + 1, PANEL):
+                cols[i] = cols[i] - m * heads[i - j]
+            head = jnp.where(lane[:1] == j, 1.0, p[j : j + 1, :])
+            p = jnp.where((lane == j) & (sub > j), 0.0, p) - m * head
+        pivot = jnp.concatenate(pivots, axis=0)
+        rs = lax.rsqrt(pivot)
+        rs = rs * (1.5 - 0.5 * pivot * rs * rs)
+        p = jnp.where(lane == sub, 1.0, p) * rs
+        y = jnp.where((lane < PANEL) & (lane > sub), 0.0, p)
+        lead = jnp.where((lane >= PANEL) & (lane < K - PANEL * k), p, 0.0)
+        lh, lm, ll = split3(lead)
         yh, ym, yl = split3(y)
         a = jnp.concatenate([lh, lh, lm, lh, ll, lm], axis=0).astype(BF)
         b = jnp.concatenate([yh, ym, yh, yl, yh, ym], axis=0).astype(BF)
-        upd = dot_f32(a, b, ((0,), (0,)))
-        new = jnp.where(col < 8, 0.0, x) - upd
-        new = jnp.where(row < K - 8 * k, new, x)
-        return pltpu.roll(jnp.concatenate([new[8:, :], y], axis=0), K - 8, axis=1)
-
-    x = lax.fori_loop(0, K // 8, step, gram)
+        new = jnp.where(col < PANEL, 0.0, x) - dot_f32(a, b, ((0,), (0,)))
+        new = jnp.where(row < K - PANEL * k, new, x)
+        return pltpu.roll(jnp.concatenate([new[PANEL:, :], y], axis=0), K - PANEL, axis=1)
+
+    x = lax.fori_loop(0, K // PANEL, step, gram)
     return jnp.where(col <= row, x, 0.0)
 
 
 def kernel(
     partial,
+    clip_ratio,
     start,
     basis_out,
-    second_out,
+    scale_out,
     summed_out,
     own,
     theirs,
@@ -109,8 +113,8 @@
     tile_send,
     tile_recv,
     start_sem,
-    end_sem,
     moved,
+    mine,
     thi,
     tlo,
     thit,
@@ -166,30 +170,38 @@
 
     partner = (1 - d, z, c)
     across = (d, z, x * 4 + (1 - yl) * 2 + co)
-    above = (d, lax.rem(z + 1, 8), c)
-    below = (d, lax.rem(z + 7, 8), c)
+
+    def dev_end_y(i):
+        return (lax.div(i, 2), z, x * 4 + lax.rem(i, 2) * 2 + co)
+
+    def dev_yz(i):
+        return (d, lax.rem(i, 8), x * 4 + lax.div(i, 8) * 2 + co)
 
     barrier = pltpu.get_barrier_semaphore()
-    peers = [partner, across, above, below]
-    peers += [dev_y(lax.rem(y + o, 4)) for o in (1, 3, 2)]
-    peers += [dev_p(lax.rem(p + o, 8)) for o in (1, 7, 2, 6, 3, 5, 4)]
+    peers = [dev_y(lax.rem(y + o, 4)) for o in (1, 3, 2)]
+    peers += [dev_end_y(lax.rem(d * 2 + yl + o, 4)) for o in (1, 3, 2)]
+    peers += [dev_yz(lax.rem(yl * 8 + z + o, 16)) for o in range(1, 16)]
     peers += [dev_j(lax.rem(j + o, 16)) for o in range(1, 16)]
     for dev in peers:
         pl.semaphore_signal(barrier, inc=1, device_id=dev, device_id_type=MESH)
+
+    def part_of(k, h, base):
+        rows = pl.ds(pl.multiple_of(k * 8, 8), 8)
+        return rows, pl.ds(pl.multiple_of(base + h * (HALF // 2), 128), HALF // 2)
 
     def own_copy(k):
         rows = pl.ds(pl.multiple_of(k * 8, 8), 8)
         mine = pl.ds(pl.multiple_of(d * HALF, HALF), HALF)
         return pltpu.make_async_copy(partial.at[rows, mine], own.at[rows, :], own_sem.at[k])
 
-    def dp_copy(k):
-        rows = pl.ds(pl.multiple_of(k * 8, 8), 8)
-        other = pl.ds(pl.multiple_of((1 - d) * HALF, HALF), HALF)
+    def dp_copy(k, turn):
+        h = lax.rem(turn + lax.div(x, 2), 2)
+        rows, other = part_of(k, h, (1 - d) * HALF)
         return pltpu.make_async_remote_copy(
             src_ref=partial.at[rows, other],
-            dst_ref=theirs.at[rows, :],
-            send_sem=dp_send.at[k],
-            recv_sem=dp_recv.at[k],
+            dst_ref=theirs.at[rows, part_of(k, h, 0)[1]],
+            send_sem=dp_send.at[2 * k + turn],
+            recv_sem=dp_recv.at[2 * k + turn],
             device_id=partner,
             device_id_type=MESH,
         )
@@ -208,7 +220,8 @@
         own_copy(k).start()
     pl.semaphore_wait(barrier, len(peers))
     for k in range(WINDOW):
-        dp_copy(k).start()
+        dp_copy(k, 0).start()
+        dp_copy(k, 1).start()
 
     @pl.when(yl == zl)
     def _():
@@ -229,33 +242,42 @@
     def chunk(k, carry):
         rows = pl.ds(pl.multiple_of(k * 8, 8), 8)
         place = pl.ds(pl.multiple_of(k * 128 + j * 8, 8), 8)
-        dp_copy(k).wait()
-
-        @pl.when(k + WINDOW < CHUNKS)
-        def _():
-            dp_copy(k + WINDOW).start()
-
-        @pl.when((k == CHUNKS - 1) & (yl == zl))
+        own_copy(k).wait()
+        for turn in (0, 1):
+            dp_copy(k, turn).wait()
+
+            @pl.when(k + WINDOW < CHUNKS)
+            def _():
+                dp_copy(k + WINDOW, turn).start()
+
+            h = lax.rem(turn + lax.div(x, 2), 2)
+            half = part_of(k, h, 0)[1]
+            summed[rows, half] = own[rows, half] + theirs[rows, half]
+
+            def block(i):
+                return summed.at[rows, pl.ds(pl.multiple_of(i * TC, 128), TC)]
+
+            def send_block(o):
+                i = h * 8 + lax.rem(j + o, 8)
+                pltpu.make_async_remote_copy(
+                    src_ref=block(i),
+                    dst_ref=tile.at[place, :],
+                    send_sem=tile_send.at[k],
+                    recv_sem=tile_recv.at[k],
+                    device_id=dev_j(i),
+                    device_id_type=MESH,
+                ).start()
+
+            if turn == 0:
+                tile[place, :] = block(j)[...]
+            else:
+                send_block(0)
+            for o in range(1, 8):
+                send_block(o)
+
+        @pl.when((k == CHUNKS - WINDOW) & (yl == zl))
         def _():
             start_across.start()
-
-        own_copy(k).wait()
-        summed[rows, :] = own[rows, :] + theirs[rows, :]
-
-        def block(i):
-            return summed.at[rows, pl.ds(pl.multiple_of(i * TC, 128), TC)]
-
-        for o in range(1, 16):
-            i = lax.rem(j + o, 16)
-            pltpu.make_async_remote_copy(
-                src_ref=block(i),
-                dst_ref=tile.at[place, :],
-                send_sem=tile_send.at[k],
-                recv_sem=tile_recv.at[k],
-                device_id=dev_j(i),
-                device_id_type=MESH,
-            ).start()
-        tile[place, :] = block(j)[...]
 
         @pl.when(k > 0)
         def _():
@@ -303,12 +325,15 @@
             i = lax.rem(me + n - o, n)
             copy(src(i), dst(i), it, base + o, base + o, dev(i)).wait()
 
+    def blocks_at(i, size):
+        return pl.ds(pl.multiple_of(i * size, 8), size)
+
     def blocks(ref, size):
         return lambda i: ref.at[pl.ds(pl.multiple_of(i * size, size), size), :]
 
     class Plane:
-        def __init__(self, it, rows, part, core_buf, x_buf, y_buf, total, sems):
-            self.it, self.rows = it, rows
+        def __init__(self, it, rows, part, core_buf, x_buf, y_buf, total, sems, y, dev_y):
+            self.it, self.rows, self.y, self.dev_y = it, rows, y, dev_y
             self.part, self.core_buf, self.x_buf, self.y_buf, self.total = part, core_buf, x_buf, y_buf, total
             self.s_core, self.s_x, self.s_y, self.s_xg, self.s_cg = sems
             self.half, self.unit = rows // 2, rows // 8
@@ -336,18 +361,18 @@
 
         def x_done(self):
             ring_wait(*self.x_args())
-            self.y_buf[self.it, y] = (self.x_buf[self.it, 0] + self.x_buf[self.it, 1]) + (
+            self.y_buf[self.it, self.y] = (self.x_buf[self.it, 0] + self.x_buf[self.it, 1]) + (
                 self.x_buf[self.it, 2] + self.x_buf[self.it, 3]
             )
 
         def y_args(self):
             return (
                 4,
-                y,
-                dev_y,
+                self.y,
+                self.dev_y,
                 self.s_y,
                 self.it,
-                lambda i: self.y_buf.at[self.it, y],
+                lambda i: self.y_buf.at[self.it, self.y],
                 lambda i: self.y_buf.at[self.it, i],
             )
 
@@ -374,11 +399,22 @@
             here = self.total.at[pl.ds(pl.multiple_of(co * self.half, self.half), self.half), :]
             return copy(here, here, self.it, self.s_cg, self.s_cg, dev_core())
 
+    class Small(Plane):
+        def mine(self):
+            return pl.ds(pl.multiple_of(co * self.half, self.half), self.half)
+
+        def x_args(self):
+            return (4, x, dev_x, self.s_x, self.it, lambda i: self.x_buf.at[self.it, x], lambda i: self.x_buf.at[self.it, i])
+
+        def x_send(self):
+            self.x_buf[self.it, x] = self.core_buf[self.it]
+            ring(*self.x_args())
+
     def left_plane(it):
-        return Plane(it, TR, lpart, lcore, lx, ly, lsum, (L_CORE, L_X, L_Y, L_XG, L_CG))
-
-    def second_plane(it):
-        return Plane(it, K, gram2, g2core, g2x, g2y, g2sum, (G2_CORE, G2_X, G2_Y, G2_XG, G2_CG))
+        return Plane(it, TR, lpart, lcore, lx, ly, lsum, (L_CORE, L_X, L_Y, L_XG, L_CG), y, dev_y)
+
+    def second_plane(it, y=y, dev_y=dev_y):
+        return Small(it, K, gram2, g2core, g2x, g2y, g2sum, (G2_CORE, G2_X, G2_Y, None, G2_CG), y, dev_y)
 
     def iteration(it, carry):
         lp, sp = left_plane(it), second_plane(it)
@@ -388,8 +424,11 @@
             gram2[...] = full_dot(right[...], right[...], ((0,), (0,)))
             sp.core_copy().start()
 
-        lpart[...] = split_product(thi[...], tlo[...], rwide[...])
-        lp.core_copy().start()
+        for half in (1 - co, co):
+            rows = pl.ds(pl.multiple_of(half * (TR // 2), TR // 2), TR // 2)
+            lpart[rows, :] = split_product(thi[rows, :], tlo[rows, :], rwide[...])
+            if half is not co:
+                lp.core_copy().start()
 
         @pl.when(it > 0)
         def _():
@@ -410,16 +449,11 @@
         @pl.when(it > 0)
         def _():
             sp.y_done()
-            sp.xg_send()
+            sp.cg_copy().start()
 
         lp.y_done()
         lp.xg_send()
 
-        @pl.when(it > 0)
-        def _():
-            sp.xg_done()
-            sp.cg_copy().start()
-
         lp.xg_done()
         lp.cg_copy().start()
 
@@ -439,22 +473,31 @@
             left[...] = full_dot(lsum[...], factor[...], ((1,), (1,)))
 
         gram1[...] = full_dot(left[...], left[...], ((0,), (0,)))
-        g1_rs = (8, p, dev_p, G1_RS, it, blocks(gram1, 16), lambda i: g1z.at[it, i])
-        g1z[it, p] = gram1[pl.ds(pl.multiple_of(p * 16, 16), 16), :]
+        half = pl.ds(pl.multiple_of(co * (K // 2), K // 2), K // 2)
+        part = gram1.at[half, :]
+        g1_rs = (8, p, dev_p, G1_RS, it, blocks(part, 8), lambda i: g1z.at[it, i])
+        g1z[it, p] = gram1[pl.ds(pl.multiple_of(co * (K // 2) + p * 8, 8), 8), :]
         ring(*g1_rs)
 
         lwide = wide(left[...])
-        wpart[...] = split_product(thit[...], tlot[...], lwide)
         w_rs = (8, p, dev_p, W_RS, it, blocks(wpart, ZB), lambda i: wz.at[it, i])
-        wz[it, p] = wpart[pl.ds(pl.multiple_of(p * ZB, 16), ZB), :]
-        ring(*w_rs)
+        for turn in (0, 1):
+            h = lax.rem(yl + turn, 2)
+            rows = pl.ds(pl.multiple_of(h * (TC // 2), TC // 2), TC // 2)
+            wpart[rows, :] = split_product(thit[rows, :], tlot[rows, :], lwide)
+            if turn == 0:
+                wz[it, p] = wpart[pl.ds(pl.multiple_of(p * ZB, 16), ZB), :]
+            for o in (0, 1, 3, 2)[1 - turn :]:
+                i = h * 4 + lax.rem(zh + o, 4)
+                far = lax.rem(i + 8 - p, 8)
+                copy(wpart.at[blocks_at(i, ZB), :], wz.at[it, p], it, W_RS + far, W_RS + far, dev_p(i)).start()
 
         ring_wait(*g1_rs)
         total = g1z[it, 0]
         for i in range(1, 8):
             total = total + g1z[it, i]
-        g1share[pl.ds(pl.multiple_of(p * 16, 16), 16), :] = total
-        share = blocks(g1share, 16)
+        g1share[pl.ds(pl.multiple_of(co * (K // 2) + p * 8, 8), 8), :] = total
+        share = blocks(g1share.at[half, :], 8)
         g1_ag = (8, p, dev_p, G1_AG, it, lambda i: share(p), share)
         ring(*g1_ag)
 
@@ -462,21 +505,67 @@
         total = wz[it, 0]
         for i in range(1, 8):
             total = total + wz[it, i]
-        right[pl.ds(pl.multiple_of(p * ZB, 16), ZB), :] = total
+
         place = blocks(right, ZB)
         w_ag = (8, p, dev_p, W_AG, it, lambda i: place(p), place)
-        ring(*w_ag)
+        end_place = blocks(moved, ZB)
+
+        def end_send(i):
+            return copy(mine, end_place(p), it, W_AG + i, W_AG + p, (d, i, x * 4 + zl * 2 + co))
+
+        def end_recv(i):
+            sender = (d, lax.rem(i, 4) * 2 + yl, x * 4 + lax.div(i, 4) * 2 + co)
+            return copy(mine, end_place(i), it, W_AG + i, W_AG + i, sender)
+
+        @pl.when(it < ITERS - 1)
+        def _():
+            right[blocks_at(p, ZB), :] = total
+            ring(*w_ag)
+
+        @pl.when(it == ITERS - 1)
+        def _():
+            mine[...] = total
+            for i in range(8):
+
+                @pl.when((i != z) | (yl != zl))
+                def _(i=i):
+                    end_send(i).start()
+
+            @pl.when(yl == zl)
+            def _():
+                moved[blocks_at(p, ZB), :] = total
 
         ring_wait(*g1_ag)
+        swap = copy(g1share.at[half, :], g1share.at[half, :], it, G1_CG, G1_CG, dev_core())
+        swap.start()
+        swap.wait()
         factor[...] = inverse_factor(g1share[...])
-        ring_wait(*w_ag)
-        right[...] = full_dot(right[...], factor[...], ((1,), (1,)))
+
+        @pl.when(it < ITERS - 1)
+        def _():
+            ring_wait(*w_ag)
+            right[...] = full_dot(right[...], factor[...], ((1,), (1,)))
+
+        @pl.when(it == ITERS - 1)
+        def _():
+            for i in range(8):
+
+                @pl.when((i != z) | (yl != zl))
+                def _(i=i):
+                    end_send(i).wait_send()
+
+                @pl.when((i != p) | (yl != zl))
+                def _(i=i):
+                    end_recv(i).wait_recv()
+
+            right[...] = full_dot(moved[...], factor[...], ((1,), (1,)))
+
         rwide[...] = wide(right[...])
         return carry
 
     lax.fori_loop(0, ITERS, iteration, 0)
 
-    sp = second_plane(ITERS)
+    sp = second_plane(ITERS, d * 2 + yl, dev_end_y)
     gram2[...] = full_dot(right[...], right[...], ((0,), (0,)))
     sp.core_copy().start()
     sp.core_done()
@@ -484,69 +573,45 @@
     sp.x_done()
     sp.y_send()
     sp.y_done()
-    sp.xg_send()
-    sp.xg_done()
     sp.cg_copy().start()
     sp.cg_copy().wait()
-    second_out[...] = g2sum[...]
-    right[...] = full_dot(right[...], inverse_factor(g2sum[...]), ((1,), (1,)))
-
-    def end_copy(i, dev):
-        rows = pl.ds(i * (TC // 2), TC // 2)
-        return pltpu.make_async_remote_copy(
-            src_ref=right.at[rows, :],
-            dst_ref=moved.at[rows, :],
-            send_sem=end_sem.at[i],
-            recv_sem=end_sem.at[2 + i],
-            device_id=dev,
-            device_id_type=MESH,
-        )
-
-    ends = [end_copy(0, above), end_copy(1, below)]
-
-    @pl.when(yl == zl)
-    def _():
-        for e in ends:
-            e.start()
-        basis_out[...] = right[...]
-        for e in ends:
-            e.wait_send()
-
-    @pl.when(yl != zl)
-    def _():
-        for e in ends:
-            e.wait_recv()
-        basis_out[...] = moved[...]
-
+    second = g2sum[...]
+    sigma = jnp.sqrt(jnp.sqrt(jnp.sum(second * second, keepdims=True)))
+    scale_out[...] = clip_ratio[...] * (math.sqrt(M) + math.sqrt(N)) / sigma
+    basis_out[...] = full_dot(right[...], inverse_factor(second), ((1,), (1,)))
     out_copy.wait()
 
 
-def power(partial, start):
+def power(partial, clip_ratio, start):
     vm = lambda *shape: pltpu.VMEM(shape, F32)
     its = ITERS + 1
     return pl.pallas_call(
         kernel,
         out_shape=(
             jax.ShapeDtypeStruct((TC, K), F32),
-            jax.ShapeDtypeStruct((K, K), F32),
+            jax.ShapeDtypeStruct((1, 1), F32),
             jax.ShapeDtypeStruct((ROWS, HALF), F32),
         ),
-        in_specs=[pl.BlockSpec(memory_space=pl.ANY)] * 2,
+        in_specs=[
+            pl.BlockSpec(memory_space=pl.ANY),
+            pl.BlockSpec(memory_space=pltpu.VMEM),
+            pl.BlockSpec(memory_space=pl.ANY),
+        ],
         out_specs=[pl.BlockSpec(memory_space=pltpu.VMEM)] * 2 + [pl.BlockSpec(memory_space=pl.ANY)],
         scratch_shapes=[
             vm(ROWS, HALF),
             vm(ROWS, HALF),
             vm(ROWS, HALF),
             vm(TR, TC),
-            pltpu.SemaphoreType.DMA((CHUNKS,)),
-            pltpu.SemaphoreType.DMA((CHUNKS,)),
+            pltpu.SemaphoreType.DMA((2 * CHUNKS,)),
+            pltpu.SemaphoreType.DMA((2 * CHUNKS,)),
             pltpu.SemaphoreType.DMA((CHUNKS,)),
             pltpu.SemaphoreType.DMA,
             pltpu.SemaphoreType.DMA((CHUNKS,)),
             pltpu.SemaphoreType.DMA((CHUNKS,)),
             pltpu.SemaphoreType.DMA((3,)),
-            pltpu.SemaphoreType.DMA((4,)),
             vm(TC, K),
+            vm(ZB, K),
             pltpu.VMEM((TR, TC), BF),
             pltpu.VMEM((TR, TC), BF),
             pltpu.VMEM((TC, TR), BF),
@@ -562,12 +627,12 @@
             vm(TC, K),
             vm(its, 8, ZB, K),
             vm(K, K),
-            vm(its, 8, 16, K),
+            vm(its, 8, 8, K),
             vm(K, K),
             vm(K, K),
             vm(its, K // 2, K),
-            vm(its, 4, K // 8, K),
-            vm(its, 4, K // 8, K),
+            vm(its, 4, K // 2, K),
+            vm(its, 4, K // 2, K),
             vm(K, K),
             vm(K, K),
             pltpu.SemaphoreType.DMA((its, SEMS)),
@@ -577,14 +642,11 @@
             collective_id=0, has_side_effects=True, vmem_limit_bytes=60 * 2**20
         ),
         name="power",
-    )(partial, start)
+    )(partial, clip_ratio, start)
 
 
 def body(partials, clip_ratio, start_block):
-    vectors, second, summed = power(partials[0], start_block)
-    sigma = jnp.sqrt(jnp.sqrt(jnp.sum(second * second)))
-    limit = clip_ratio[0] * (math.sqrt(M) + math.sqrt(N))
-    scale = limit / sigma
+    vectors, scale, summed = power(partials[0], clip_ratio.reshape(1, 1), start_block)
     update = summed * scale
     return (update, vectors)
 

time: 349 us -> 277 us (0.79)
  Pallas kernels: 336 us -> 269 us
    pallas_call x1, Pallas kernels: 336 us -> 269 us  [power(): pl.pallas_call(kernel, out_shape=(jax.ShapeDtypeStruct((TC, K), F32), jax...]
where the time goes in v3:
time: 277 us; the launch traced here: 276 us
  Pallas kernels  269 us (97%)
  other arithmetic  4.86 us (2%)
    pallas_call x1, Pallas kernels, power(): pl.pallas_call(kernel, out_shape=(jax.ShapeDtypeStruct((TC, K), F32), jax...  269 us

profile of v3, /device:TPU:1, one launch (start us, length us, event | category | flops | bytes accessed | tf_op | source)
XLA Modules:
  0.0 276.3 jit_solution(5003102111130567035)
XLA Ops:
  1.3 269.4 %power.1 = (f32[896,128]{1,0:T(8,128)}, f32[1,1]{1,0:T(1,128)}, f32[64,14336]{1,0:T(8,128)}) custom-call(f32[64,28672]{1,0:T(8,128)} %bitcast.4, f32[1,1]{1,0:T(1,128)} %bitcast.3.clip_ratio, f32[896,128]{1,0:T(8,128)} %start.1), custom_call_target="tpu_custom_call" | custom-call | tf_op jit(solution)/shard_map/power/pallas_call | solution.py:588
  270.6 0.0 copy-start
  270.6 4.9 %broadcast_multiply_fusion = f32[64,14336]{1,0:T(8,128)} fusion(f32[64,14336]{1,0:T(8,128)} %get-tuple-element.5, f32[]{:T(128)} %bitcast.2), kind=kLoop, calls=%fused_computation | loop fusion | flops 917504 | bytes 7340036 | tf_op jit(solution)/shard_map/mul | solution.py:650
  275.5 0.0 copy-done
  275.5 0.8 copy.7
Async XLA Ops:
  270.6 4.9 %copy-start = (f32[896,128]{1,0:T(8,128)S(1)}, f32[896,128]{1,0:T(8,128)}, u32[]{:S(2)}) copy-start(f32[896,128]{1,0:T(8,128)} %get-tuple-element.11) | copy-start | bytes 1376260

commit v4 on v3

--- a/solution.py
+++ b/solution.py
@@ -17,6 +17,7 @@
 HALF = N // 2
 CHUNKS = 8
 PANEL = 16
+START_AT = 4
 WINDOW = 2
 ZB = 112
 MESH = pl.DeviceIdType.MESH
@@ -97,10 +98,9 @@
 
 def kernel(
     partial,
-    clip_ratio,
     start,
-    basis_out,
-    scale_out,
+    right_out,
+    second_out,
     summed_out,
     own,
     theirs,
@@ -207,25 +207,40 @@
         )
 
     start_here = pltpu.make_async_copy(start, right, start_sem.at[0])
-    start_across = pltpu.make_async_remote_copy(
-        src_ref=start,
-        dst_ref=right,
-        send_sem=start_sem.at[1],
-        recv_sem=start_sem.at[2],
-        device_id=across,
-        device_id_type=MESH,
-    )
+
+    def quarter(i):
+        return pl.ds(pl.multiple_of(i * (TC // 4), 8), TC // 4)
+
+    def start_copy(src, i, out, into, dev):
+        return pltpu.make_async_remote_copy(
+            src_ref=src.at[quarter(i), :],
+            dst_ref=right.at[quarter(i), :],
+            send_sem=start_sem.at[out],
+            recv_sem=start_sem.at[into],
+            device_id=dev,
+            device_id_type=MESH,
+        )
+
+    start_across = start_copy(start, zh, 1, 2, across)
+
+    def start_relay(o):
+        return start_copy(right, zh, 2 + o, 5 + o, (d, lax.rem(zh + o, 4) * 2 + zl, c))
+
+    def start_relayed(o):
+        return start_copy(right, lax.rem(zh + 4 - o, 4), 2 + o, 5 + o, across)
 
     for k in range(CHUNKS):
         own_copy(k).start()
     pl.semaphore_wait(barrier, len(peers))
+
+    @pl.when(yl == zl)
+    def _():
+        start_across.start()
+        start_here.start()
+
     for k in range(WINDOW):
         dp_copy(k, 0).start()
         dp_copy(k, 1).start()
-
-    @pl.when(yl == zl)
-    def _():
-        start_here.start()
 
     def prepare(k):
         rows = pl.ds(pl.multiple_of(k * 128, 128), 128)
@@ -239,6 +254,10 @@
         thit[:, rows] = hi
         tlot[:, rows] = lo
 
+    def first_product(k):
+        rows = pl.ds(pl.multiple_of(k * 128, 128), 128)
+        lpart[rows, :] = split_product(thi[rows, :], tlo[rows, :], rwide[...])
+
     def chunk(k, carry):
         rows = pl.ds(pl.multiple_of(k * 8, 8), 8)
         place = pl.ds(pl.multiple_of(k * 128 + j * 8, 8), 8)
@@ -275,13 +294,37 @@
             for o in range(1, 8):
                 send_block(o)
 
-        @pl.when((k == CHUNKS - WINDOW) & (yl == zl))
-        def _():
-            start_across.start()
+        @pl.when((k == 0) & (yl != zl))
+        def _():
+            start_across.wait_recv()
+            for o in (1, 3, 2):
+                start_relay(o).start()
+
+        @pl.when(k == START_AT)
+        def _():
+            @pl.when(yl == zl)
+            def _():
+                start_here.wait()
+                start_across.wait_send()
+
+            @pl.when(yl != zl)
+            def _():
+                for o in (1, 3, 2):
+                    start_relay(o).wait_send()
+                    start_relayed(o).wait_recv()
+
+            right[...] = right[...] * math.sqrt(3.0 / N)
+            rwide[...] = wide(right[...])
+            for i in range(START_AT - 1):
+                first_product(i)
 
         @pl.when(k > 0)
         def _():
             prepare(k - 1)
+
+        @pl.when(k >= START_AT)
+        def _():
+            first_product(k - 1)
 
         return carry
 
@@ -289,21 +332,10 @@
     out_copy = pltpu.make_async_copy(summed, summed_out, out_sem)
     out_copy.start()
     prepare(CHUNKS - 1)
+    first_product(CHUNKS - 1)
     for k in range(CHUNKS):
         sent = tile.at[pl.ds(0, 120), :]
         pltpu.make_async_copy(sent, sent, tile_send.at[k]).wait()
-
-    @pl.when(yl == zl)
-    def _():
-        start_here.wait()
-        start_across.wait_send()
-
-    @pl.when(yl != zl)
-    def _():
-        start_across.wait_recv()
-
-    right[...] = right[...] * math.sqrt(3.0 / N)
-    rwide[...] = wide(right[...])
 
     def copy(src, dst, it, slot_out, slot_in, dev):
         return pltpu.make_async_remote_copy(
@@ -426,7 +458,11 @@
 
         for half in (1 - co, co):
             rows = pl.ds(pl.multiple_of(half * (TR // 2), TR // 2), TR // 2)
-            lpart[rows, :] = split_product(thi[rows, :], tlo[rows, :], rwide[...])
+
+            @pl.when(it > 0)
+            def _(rows=rows):
+                lpart[rows, :] = split_product(thi[rows, :], tlo[rows, :], rwide[...])
+
             if half is not co:
                 lp.core_copy().start()
 
@@ -575,26 +611,23 @@
     sp.y_done()
     sp.cg_copy().start()
     sp.cg_copy().wait()
-    second = g2sum[...]
-    sigma = jnp.sqrt(jnp.sqrt(jnp.sum(second * second, keepdims=True)))
-    scale_out[...] = clip_ratio[...] * (math.sqrt(M) + math.sqrt(N)) / sigma
-    basis_out[...] = full_dot(right[...], inverse_factor(second), ((1,), (1,)))
+    second_out[...] = g2sum[...]
+    right_out[...] = right[...]
     out_copy.wait()
 
 
-def power(partial, clip_ratio, start):
+def power(partial, start):
     vm = lambda *shape: pltpu.VMEM(shape, F32)
     its = ITERS + 1
     return pl.pallas_call(
         kernel,
         out_shape=(
             jax.ShapeDtypeStruct((TC, K), F32),
-            jax.ShapeDtypeStruct((1, 1), F32),
+            jax.ShapeDtypeStruct((K, K), F32),
             jax.ShapeDtypeStruct((ROWS, HALF), F32),
         ),
         in_specs=[
             pl.BlockSpec(memory_space=pl.ANY),
-            pl.BlockSpec(memory_space=pltpu.VMEM),
             pl.BlockSpec(memory_space=pl.ANY),
         ],
         out_specs=[pl.BlockSpec(memory_space=pltpu.VMEM)] * 2 + [pl.BlockSpec(memory_space=pl.ANY)],
@@ -609,7 +642,7 @@
             pltpu.SemaphoreType.DMA,
             pltpu.SemaphoreType.DMA((CHUNKS,)),
             pltpu.SemaphoreType.DMA((CHUNKS,)),
-            pltpu.SemaphoreType.DMA((3,)),
+            pltpu.SemaphoreType.DMA((9,)),
             vm(TC, K),
             vm(ZB, K),
             pltpu.VMEM((TR, TC), BF),
@@ -642,13 +675,54 @@
             collective_id=0, has_side_effects=True, vmem_limit_bytes=60 * 2**20
         ),
         name="power",
-    )(partial, clip_ratio, start)
+    )(partial, start)
+
+
+def finish_kernel(summed, right, second, clip_ratio, update_out, basis_out, block, vectors, in_sem, out_sem, right_sem):
+    def into(k):
+        return pltpu.make_async_copy(summed.at[pl.ds(k * 8, 8), :], block.at[pl.ds(k * 8, 8), :], in_sem.at[k])
+
+    def out(k):
+        return pltpu.make_async_copy(block.at[pl.ds(k * 8, 8), :], update_out.at[pl.ds(k * 8, 8), :], out_sem.at[k])
+
+    right_copy = pltpu.make_async_copy(right, vectors, right_sem)
+    for k in range(CHUNKS):
+        into(k).start()
+    right_copy.start()
+    sigma = jnp.sqrt(jnp.sqrt(jnp.sum(second[...] * second[...], keepdims=True)))
+    scale = clip_ratio[...] * (math.sqrt(M) + math.sqrt(N)) / sigma
+    for k in range(CHUNKS):
+        into(k).wait()
+        block[k * 8 : (k + 1) * 8, :] = block[k * 8 : (k + 1) * 8, :] * scale
+        out(k).start()
+    factor = inverse_factor(second[...])
+    right_copy.wait()
+    basis_out[...] = full_dot(vectors[...], factor, ((1,), (1,)))
+    for k in range(CHUNKS):
+        out(k).wait()
+
+
+def finish(summed, right, second, clip_ratio):
+    return pl.pallas_call(
+        finish_kernel,
+        out_shape=(jax.ShapeDtypeStruct((ROWS, HALF), F32), jax.ShapeDtypeStruct((TC, K), F32)),
+        in_specs=[pl.BlockSpec(memory_space=pl.ANY)] * 2 + [pl.BlockSpec(memory_space=pltpu.VMEM)] * 2,
+        out_specs=(pl.BlockSpec(memory_space=pl.ANY), pl.BlockSpec(memory_space=pltpu.VMEM)),
+        scratch_shapes=[
+            pltpu.VMEM((ROWS, HALF), F32),
+            pltpu.VMEM((TC, K), F32),
+            pltpu.SemaphoreType.DMA((CHUNKS,)),
+            pltpu.SemaphoreType.DMA((CHUNKS,)),
+            pltpu.SemaphoreType.DMA,
+        ],
+        compiler_params=pltpu.CompilerParams(vmem_limit_bytes=60 * 2**20),
+        name="finish",
+    )(summed, right, second, clip_ratio)
 
 
 def body(partials, clip_ratio, start_block):
-    vectors, scale, summed = power(partials[0], clip_ratio.reshape(1, 1), start_block)
-    update = summed * scale
-    return (update, vectors)
+    right, second, summed = power(partials[0], start_block)
+    return finish(summed, right, second, clip_ratio.reshape(1, 1))
 
 
 def solution(mesh):

time: 277 us -> 273 us (0.986)
  other arithmetic: 4.86 us -> 0 us
    pallas_call x0 -> x1, Pallas kernels: none -> 8.66 us  [finish(): pl.pallas_call(finish_kernel, out_shape=(jax.ShapeDtypeStruct((ROWS, HALF...]
    pallas_call x1, Pallas kernels: 269 us -> 262 us  [power(): pl.pallas_call(kernel, out_shape=(jax.ShapeDtypeStruct((TC, K), F32), jax...]
    mul x1 -> x0, other arithmetic: 4.86 us -> none  [body(): update = summed * scale]
where the time goes in v4:
time: 273 us; the launch traced here: 272 us
  Pallas kernels  270 us (99%)
    pallas_call x1, Pallas kernels, power(): pl.pallas_call(kernel, out_shape=(jax.ShapeDtypeStruct((TC, K), F32), jax...  262 us
    pallas_call x1, Pallas kernels, finish(): pl.pallas_call(finish_kernel, out_shape=(jax.ShapeDtypeStruct((ROWS, HALF...  8.66 us

profile of v4, /device:TPU:1, one launch (start us, length us, event | category | flops | bytes accessed | tf_op | source)
XLA Modules:
  0.0 271.7 jit_solution(3363630871293303811)
XLA Ops:
  1.3 261.8 %power.1 = (f32[896,128]{1,0:T(8,128)}, f32[128,128]{1,0:T(8,128)}, f32[64,14336]{1,0:T(8,128)}) custom-call(f32[64,28672]{1,0:T(8,128)} %bitcast.3, f32[896,128]{1,0:T(8,128)} %start.1), custom_call_target="tpu_custom_call" | custom-call | tf_op jit(solution)/shard_map/power/pallas_call | solution.py:622
  263.1 8.7 %finish.1 = (f32[64,14336]{1,0:T(8,128)}, f32[896,128]{1,0:T(8,128)}) custom-call(f32[64,14336]{1,0:T(8,128)} %get-tuple-element.5.summed, f32[896,128]{1,0:T(8,128)} %get-tuple-element.6.right, f32[128,128]{1,0:T(8,128)} %get-tuple-element.7.second, f32[1,1]{1,0:T(1,128)} %bitcast.2.clip_ratio), custom_call_target="tpu_custom_call" | custom-call | tf_op jit(solution)/shard_map/finish/pallas_call | solution.py:706

commit v5 on v4

--- a/solution.py
+++ b/solution.py
@@ -21,6 +21,7 @@
 WINDOW = 2
 ZB = 112
 MESH = pl.DeviceIdType.MESH
+FAR_FIRST = {4: (2, 1, 3), 8: (6, 2, 5, 7, 1, 3, 4)}
 BF = jnp.bfloat16
 F32 = jnp.float32
 
@@ -348,12 +349,12 @@
         )
 
     def ring(n, me, dev, base, it, src, dst):
-        for o in sorted(range(1, n), key=lambda o: min(o, n - o)):
+        for o in FAR_FIRST[n]:
             i = lax.rem(me + o, n)
             copy(src(i), dst(me), it, base + o, base + o, dev(i)).start()
 
     def ring_wait(n, me, dev, base, it, src, dst):
-        for o in sorted(range(1, n), key=lambda o: min(o, n - o)):
+        for o in FAR_FIRST[n]:
             i = lax.rem(me + n - o, n)
             copy(src(i), dst(i), it, base + o, base + o, dev(i)).wait()
 
@@ -490,14 +491,13 @@
         lp.y_done()
         lp.xg_send()
 
+        @pl.when(it > 0)
+        def _():
+            sp.cg_copy().wait()
+            factor[...] = inverse_factor(g2sum[...])
+
         lp.xg_done()
         lp.cg_copy().start()
-
-        @pl.when(it > 0)
-        def _():
-            sp.cg_copy().wait()
-            factor[...] = inverse_factor(g2sum[...])
-
         lp.cg_copy().wait()
 
         @pl.when(it == 0)
@@ -518,12 +518,12 @@
         lwide = wide(left[...])
         w_rs = (8, p, dev_p, W_RS, it, blocks(wpart, ZB), lambda i: wz.at[it, i])
         for turn in (0, 1):
-            h = lax.rem(yl + turn, 2)
+            h = lax.rem(yl + 1 - turn, 2)
             rows = pl.ds(pl.multiple_of(h * (TC // 2), TC // 2), TC // 2)
             wpart[rows, :] = split_product(thit[rows, :], tlot[rows, :], lwide)
-            if turn == 0:
+            if turn == 1:
                 wz[it, p] = wpart[pl.ds(pl.multiple_of(p * ZB, 16), ZB), :]
-            for o in (0, 1, 3, 2)[1 - turn :]:
+            for o in (2, 1, 3, 0)[: 4 - turn]:
                 i = h * 4 + lax.rem(zh + o, 4)
                 far = lax.rem(i + 8 - p, 8)
                 copy(wpart.at[blocks_at(i, ZB), :], wz.at[it, p], it, W_RS + far, W_RS + far, dev_p(i)).start()

time: 273 us -> 266 us (0.974)
  Pallas kernels: 270 us -> 264 us
    pallas_call x1, Pallas kernels: 262 us -> 255 us  [power(): pl.pallas_call(kernel, out_shape=(jax.ShapeDtypeStruct((TC, K), F32), jax...]
where the time goes in v5:
time: 266 us; the launch traced here: 265 us
  Pallas kernels  264 us (99%)
    pallas_call x1, Pallas kernels, power(): pl.pallas_call(kernel, out_shape=(jax.ShapeDtypeStruct((TC, K), F32), jax...  255 us
    pallas_call x1, Pallas kernels, finish(): pl.pallas_call(finish_kernel, out_shape=(jax.ShapeDtypeStruct((ROWS, HALF...  8.66 us

profile of v5, /device:TPU:1, one launch (start us, length us, event | category | flops | bytes accessed | tf_op | source)
XLA Modules:
  0.0 265.0 jit_solution(11257610544749806982)
XLA Ops:
  1.3 255.1 %power.1 = (f32[896,128]{1,0:T(8,128)}, f32[128,128]{1,0:T(8,128)}, f32[64,14336]{1,0:T(8,128)}) custom-call(f32[64,28672]{1,0:T(8,128)} %bitcast.3, f32[896,128]{1,0:T(8,128)} %start.1), custom_call_target="tpu_custom_call" | custom-call | tf_op jit(solution)/shard_map/power/pallas_call | solution.py:622
  256.4 8.7 %finish.1 = (f32[64,14336]{1,0:T(8,128)}, f32[896,128]{1,0:T(8,128)}) custom-call(f32[64,14336]{1,0:T(8,128)} %get-tuple-element.5.summed, f32[896,128]{1,0:T(8,128)} %get-tuple-element.6.right, f32[128,128]{1,0:T(8,128)} %get-tuple-element.7.second, f32[1,1]{1,0:T(1,128)} %bitcast.2.clip_ratio), custom_call_target="tpu_custom_call" | custom-call | tf_op jit(solution)/shard_map/finish/pallas_call | solution.py:706
